TPU v7x, 512 devices: a whole 4x4x16 slice. The times are simulated.
512 devices in a mesh: batch: 32 (over z, core), mp: 16 (over y, x).
Axes of the slice: x: 4, y: 4, z: 16, core: 2. Of those that a mesh axis runs over, the one named last changes fastest.
Arguments:
- queries: bfloat16 [512, 16384], P('batch', 'mp'), may hold values from -384 to 384, as said below
- prompt_cache: bfloat16 [32, 16, 4096, 256], P('batch', 'mp'), may hold values from -48 to 48, as said below
- pool: bfloat16 [1024, 16, 64, 256], P('batch', 'mp'), may hold values from -48 to 48, as said below
- block_table: int32 [512, 4], replicated, may hold values from 0 to 1023, as said below
- parents: int32 [512], replicated, may hold values from 0 to 511, as said below
- lengths: int32 [32], P('batch'), may hold values from 2048 to 8192, as said below
Outputs:
- attended: float32 [512, 16384], P('batch', 'mp')
Inputs may be any that keep to these rules, and one draw needn't show every extreme that they name: `queries`: custom float draw of activations; entries stay within the range. `prompt_cache`: keys are of order one and values about eight times larger. `pool`: keys are of order one and values larger, as in prompt_cache. `block_table`: block b is held by batch index b // 32. A row's 4 entries are distinct. The rows of one request name at most 2 distinct blocks held by any one batch index, and exactly 2 held by some index. parents[i] // 16 == i // 16: a row continues a beam of its own request. `lengths`: some request has 8192 valid prompt tokens.
All inputs are finite; a program needn't handle non-finite values.
Results may differ from a plain program's by a relative error of at most 0.007.
Values may be sent and summed in bfloat16 or wider, within the bound.
A program may use at most 64 MiB of HBM per device.

v0:
```python
import jax
import jax.numpy as jnp
from jax import lax
from jax.sharding import PartitionSpec as P

HD = 128
GROUP = 16
BEAMS = 16
SUF = 4


big_negative = -1e30


def swapped(value, axis, stride):
    mask = 2**stride
    pairs = [(source, source ^ mask) for source in range(lax.axis_size(axis))]
    return lax.ppermute(value, axis, pairs)


def partial_softmax(scores, keep, values):
    top = jnp.max(jnp.where(keep, scores, big_negative), axis=-1)
    weights = jnp.where(keep, jnp.exp(scores - top[..., None]), 0.0)
    total = jnp.sum(weights, axis=-1)
    summed = jnp.dot(weights.astype(jnp.bfloat16), values, preferred_element_type=jnp.float32)
    return (top, total, summed)


def combine(first, second):
    top = jnp.maximum(first[0], second[0])
    scale_a = jnp.exp(first[0] - top)
    scale_b = jnp.exp(second[0] - top)
    total = first[1] * scale_a + second[1] * scale_b
    summed = first[2] * scale_a[..., None] + second[2] * scale_b[..., None]
    return (top, total, summed)


def pick_slots(wanted, slot_ids, capacity):
    hit = jnp.any(wanted[:, :, None] == slot_ids[:, None, :], axis=1)
    rank = jnp.cumsum(hit.astype(jnp.int32), axis=1) - 1
    order = jnp.arange(capacity, dtype=jnp.int32)
    chosen = hit[:, None, :] & (rank[:, None, :] == order[None, :, None])
    positions = jnp.arange(slot_ids.shape[1], dtype=jnp.int32)
    local_index = jnp.sum(jnp.where(chosen, positions[None, None, :], 0), axis=2)
    global_ids = jnp.sum(jnp.where(chosen, slot_ids[:, None, :], 0), axis=2)
    present = jnp.any(chosen, axis=2)
    return (local_index, global_ids, present)


def on_device(queries, prompt_cache, pool, block_table, parents, lengths):
    n_batch = lax.axis_size("batch")
    myself = lax.axis_index("batch")
    parity = lax.axis_index("mp") % 2
    ndist = 2 ** (SUF + 1) - 2
    capacity = 2 * ((ndist // 2 + n_batch - 1) // n_batch)
    half = pool.shape[2]
    slots = pool.shape[0]
    scale = HD ** (-0.5)
    vec_rows = BEAMS * GROUP
    own = queries.reshape(BEAMS, GROUP // 2, HD)
    other = swapped(queries, "mp", 0).reshape(BEAMS, GROUP // 2, HD)
    lower = jnp.where(parity == 0, own, other)
    upper = jnp.where(parity == 0, other, own)
    vectors = jnp.concatenate([lower, upper], axis=1).reshape(vec_rows, HD)
    prompt_rows = prompt_cache[0, 0]
    token = jnp.arange(prompt_rows.shape[0], dtype=jnp.int32)
    position = token // half * (2 * half) + parity * half + token % half
    keep_prompt = (position < lengths[0])[None, :]
    prompt_scores = (
        jnp.einsum("qd,td->qt", vectors, prompt_rows[:, :HD], preferred_element_type=jnp.float32)
        * scale
    )
    prompt_part = partial_softmax(prompt_scores, keep_prompt, prompt_rows[:, HD:])
    referenced = block_table[parents]
    mine = lax.dynamic_slice_in_dim(referenced, myself * BEAMS, BEAMS, 0)
    by_dest = referenced.reshape(n_batch, BEAMS * SUF)
    held = jnp.broadcast_to(
        myself * slots + jnp.arange(slots, dtype=jnp.int32)[None, :], (n_batch, slots)
    )
    send_local, send_ids, send_present = pick_slots(by_dest, held, capacity)
    outgoing = pool[:, 0][send_local]
    incoming = lax.all_to_all(outgoing, "batch", split_axis=0, concat_axis=0, tiled=True)
    owner_slots = (
        jnp.arange(n_batch, dtype=jnp.int32)[:, None] * slots
        + jnp.arange(slots, dtype=jnp.int32)[None, :]
    )
    wanted = jnp.broadcast_to(mine.reshape(1, BEAMS * SUF), (n_batch, BEAMS * SUF))
    got_local, got_ids, got_present = pick_slots(wanted, owner_slots, capacity)
    member = jnp.any(mine[:, :, None] == got_ids.reshape(1, 1, -1), axis=1) & got_present.reshape(
        1, -1
    )
    flat = incoming.reshape(n_batch * capacity * half, 2 * HD)
    suffix_scores = (
        jnp.einsum("qd,td->qt", vectors, flat[:, :HD], preferred_element_type=jnp.float32) * scale
    )
    keep_suffix = jnp.broadcast_to(
        member[:, None, :, None], (BEAMS, GROUP, n_batch * capacity, half)
    )
    keep_suffix = keep_suffix.reshape(vec_rows, n_batch * capacity * half)
    suffix_part = partial_softmax(suffix_scores, keep_suffix, flat[:, HD:])
    top, total, summed = combine(prompt_part, suffix_part)
    top = top.reshape(BEAMS, GROUP)
    total = total.reshape(BEAMS, GROUP)
    summed = summed.reshape(BEAMS, GROUP, HD)
    split = GROUP // 2
    kept = (
        jnp.where(parity == 0, top[:, :split], top[:, split:]),
        jnp.where(parity == 0, total[:, :split], total[:, split:]),
        jnp.where(parity == 0, summed[:, :split], summed[:, split:]),
    )
    given = (
        jnp.where(parity == 0, top[:, split:], top[:, :split]),
        jnp.where(parity == 0, total[:, split:], total[:, :split]),
        jnp.where(parity == 0, summed[:, split:], summed[:, :split]),
    )
    received = swapped((given[0], given[1], given[2]), "mp", 0)
    final = combine(kept, received)
    return (final[2] / final[1][..., None]).reshape(BEAMS, split * HD)


def solution(mesh):
    return jax.shard_map(
        on_device,
        mesh=mesh,
        in_specs=(
            P("batch", "mp"),
            P("batch", "mp", None, None),
            P("batch", "mp", None, None),
            P(),
            P(),
            P("batch"),
        ),
        out_specs=P("batch", "mp"),
        check_vma=False,
    )
```

profile of v0, /device:TPU:24, one launch (start us, length us, event | category | flops | bytes accessed | tf_op | source)
XLA Modules:
  0.0 147.4 jit_solution(13513599611002975200)
XLA Ops:
  0.0 0.9 copy.11
  0.9 0.7 compare_select_fusion
  1.6 1.0 gather_fusion
  2.8 0.7 compare_reduce_fusion
  3.5 0.2 reduce_window_sum.18
  4.1 2.0 %gather_fusion.1 = bf16[64,64,256]{2,1,0:T(8,128)(2,1)} fusion(bf16[32,64,256]{2,1,0:T(8,128)(2,1)S(1)} %bitcast.26, s32[1024]{0:T(1024)S(1)} %pad_clamp_fusion), kind=kCustom, calls=%fused_computation.1 | custom fusion | bytes 4194560 | tf_op jit(solution)/shard_map/gather | solution.py:81
  6.1 15.6 %all-to-all-start = ((bf16[32,2,64,256]{3,2,1,0:T(8,128)(2,1)}), bf16[32,2,64,256]{3,2,1,0:T(8,128)(2,1)}, u32[]{:S(2)}, u32[]{:S(2)}) async-start(bf16[32,2,64,256]{3,2,1,0:T(8,128)(2,1)} %bitcast.5), calls=%async_computation | async-start | bytes 4194304 | tf_op jit(solution)/shard_map/all_to_all | solution.py:82
  21.7 3.4 %collective-permute-start = (bf16[16,1024]{1,0:T(8,128)(2,1)S(1)}, bf16[16,1024]{1,0:T(8,128)(2,1)S(1)}, u32[]{:S(2)}, u32[]{:S(2)}) collective-permute-start(bf16[16,1024]{1,0:T(8,128)(2,1)S(1)} %copy-done.2), channel_id=1, source_target_pairs={{0,1},{1,0},{2,3},{3,2},{4,5},{5,4},{6,7},{7,6},{8,9},{9,8},{10,11... | collective-permute-start | bytes 98312 | tf_op jit(solution)/shard_map/ppermute | solution.py:18
  25.4 0.8 compare_reduce_fusion.1
  26.2 0.2 reduce_window_sum.17
  27.9 2.0 %broadcast_in_dim.80 = pred[16,16,64,64]{3,2,1,0:T(32,128)(4,1)} broadcast(pred[16,64]{1,0:T(8,128)(4,1)S(1)} %broadcast_and_fusion), dimensions={0,2} | broadcast | bytes 1049600 | tf_op jit(solution)/shard_map/broadcast_in_dim | solution.py:96
  29.8 6.2 %reshape.159 = pred[256,4096]{1,0:T(32,128)(4,1)S(1)} reshape(pred[16,16,64,64]{3,2,1,0:T(32,128)(4,1)} %broadcast_in_dim.80) | data formatting | bytes 2097152 | tf_op jit(solution)/shard_map/reshape | solution.py:99
  36.1 3.9 %select_reduce_fusion.1 = (f32[256]{0:T(256)S(1)}, f32[256,4096]{1,0:T(8,128)}) fusion(pred[4096]{0:T(1024)(128)(4,1)S(1)} %fusion.38, bf16[256,128]{1,0:T(8,128)(2,1)S(1)} %bitcast.27, bf16[4096,256]{1,0:T(8,128)(2,1)} %bitcast.29), kind=kOutput, calls=%fused_computation.7 | convolution fusion | flops 271580928 | bytes 5313536 | tf_op jit(solution)/shard_map/qd,td->qt/dot_general | solution.py:70
  40.1 3.1 %fusion = f32[256]{0:T(256)S(1)} fusion(f32[256,4096]{1,0:T(8,128)} %get-tuple-element.17, f32[256]{0:T(256)S(1)} %get-tuple-element.16, pred[4096]{0:T(1024)(128)(4,1)S(1)} %fusion.38), kind=kLoop, calls=%fused_computation.8 | loop fusion | flops 3145472 | bytes 4200448 | tf_op jit(solution)/shard_map/reduce_sum | solution.py:24
  43.2 77.7 %all-to-all-done = bf16[32,2,64,256]{3,2,1,0:T(8,128)(2,1)} async-done(((bf16[32,2,64,256]{3,2,1,0:T(8,128)(2,1)}), bf16[32,2,64,256]{3,2,1,0:T(8,128)(2,1)}, u32[]{:S(2)}, u32[]{:S(2)}) %all-to-all-start) | async-done | bytes 2097184 | tf_op jit(solution)/shard_map/all_to_all | solution.py:82
  120.9 4.1 %select_reduce_fusion = (f32[256]{0:T(256)S(1)}, f32[256,4096]{1,0:T(8,128)}) fusion(pred[256,4096]{1,0:T(32,128)(4,1)S(1)} %reshape.159, bf16[256,128]{1,0:T(8,128)(2,1)S(1)} %bitcast.28, bf16[4096,256]{1,0:T(8,128)(2,1)} %bitcast.6), kind=kOutput, calls=%fused_computation.5 | convolution fusion | flops 271580928 | bytes 6358016 | tf_op jit(solution)/shard_map/qd,td->qt/dot_general | solution.py:94
  125.2 3.4 %fusion.2 = f32[256]{0:T(256)S(1)} fusion(pred[256,4096]{1,0:T(32,128)(4,1)S(1)} %reshape.159, f32[256,4096]{1,0:T(8,128)} %get-tuple-element.15, f32[256]{0:T(256)S(1)} %get-tuple-element.14), kind=kLoop, calls=%fused_computation.10 | loop fusion | flops 3145472 | bytes 5244928 | tf_op jit(solution)/shard_map/reduce_sum | solution.py:24
  128.6 2.4 %fusion.19 = f32[256,128]{1,0:T(8,128)S(1)} fusion(pred[256,4096]{1,0:T(32,128)(4,1)S(1)} %reshape.159, f32[256,4096]{1,0:T(8,128)S(1)} %copy-done.1, f32[256]{0:T(256)S(1)} %get-tuple-element.14, bf16[4096,256]{1,0:T(8,128)(2,1)} %bitcast.6, f32[256]{0:T(256)S(1)} %get-tuple-element.13), kind=kOutput, calls=%fused_computation.21 | convolution fusion | flops 271613952 | bytes 6424576 | tf_op jit(solution)/shard_map/dot_general | solution.py:25
  131.2 3.4 %collective-permute-start.3 = (f32[16,8]{1,0:T(8,128)S(1)}, f32[16,8]{1,0:T(8,128)S(1)}, u32[]{:S(2)}, u32[]{:S(2)}) collective-permute-start(f32[16,8]{1,0:T(8,128)S(1)} %slice_select_fusion.1), channel_id=1, source_target_pairs={{0,1},{1,0},{2,3},{3,2},{4,5},{5,4},{6,7},{7,6},{8,9},{9,8},{10,11... | collective-permute-start | bytes 1544 | tf_op jit(solution)/shard_map/ppermute | solution.py:18
  134.7 2.4 %collective-permute-start.1 = (f32[16,8]{1,0:T(8,128)S(1)}, f32[16,8]{1,0:T(8,128)S(1)}, u32[]{:S(2)}, u32[]{:S(2)}) collective-permute-start(f32[16,8]{1,0:T(8,128)S(1)} %slice_select_fusion.2), channel_id=1, source_target_pairs={{0,1},{1,0},{2,3},{3,2},{4,5},{5,4},{6,7},{7,6},{8,9},{9,8},{10,11... | collective-permute-start | bytes 1544 | tf_op jit(solution)/shard_map/ppermute | solution.py:18
  137.1 3.3 %fusion.16 = f32[256,128]{1,0:T(8,128)S(1)} fusion(f32[256,128]{1,0:T(8,128)S(1)} %fusion.19, f32[256,4096]{1,0:T(8,128)} %get-tuple-element.17, f32[256]{0:T(256)S(1)} %get-tuple-element.16, pred[4096]{0:T(1024)(128)(4,1)S(1)} %fusion.38, bf16[4096,256]{1,0:T(8,128)(2,1)} %bitcast.30, f32[256]{0:T(256)S(1)} %get-tuple-element.12), kind=kOutput, calls=%fused_computation.20 | convolution fusion | flops 271646720 | bytes 5511168 | tf_op jit(solution)/shard_map/dot_general | solution.py:25
  140.4 3.4 %collective-permute-start.2 = (f32[16,8,128]{2,1,0:T(8,128)S(1)}, f32[16,8,128]{2,1,0:T(8,128)S(1)}, u32[]{:S(2)}, u32[]{:S(2)}) collective-permute-start(f32[16,8,128]{2,1,0:T(8,128)S(1)} %slice_select_fusion), channel_id=1, source_target_pairs={{0,1},{1,0},{2,3},{3,2},{4,5},{5,4},{6,7},{7,6},{8,9},{9,8},{10,11... | collective-permute-start | bytes 196616 | tf_op jit(solution)/shard_map/ppermute | solution.py:18
  144.0 2.6 %collective-permute-done.2 = f32[16,8,128]{2,1,0:T(8,128)S(1)} collective-permute-done((f32[16,8,128]{2,1,0:T(8,128)S(1)}, f32[16,8,128]{2,1,0:T(8,128)S(1)}, u32[]{:S(2)}, u32[]{:S(2)}) %collective-permute-start.2) | collective-permute-done | bytes 65568 | tf_op jit(solution)/shard_map/ppermute | solution.py:18
  146.7 0.6 copy.20
  (50 shorter events, 2.3 us)
Async XLA Ops:
  0.0 4.1 %copy-start = (bf16[32,1,64,256]{3,2,1,0:T(8,128)(2,1)S(1)}, bf16[32,1,64,256]{3,2,1,0:T(8,128)(2,1)}, u32[]{:S(2)}) copy-start(bf16[32,1,64,256]{3,2,1,0:T(8,128)(2,1)} %param.8) | copy-start | bytes 3145732
  4.1 17.6 %copy-start.2 = (bf16[16,1024]{1,0:T(8,128)(2,1)S(1)}, bf16[16,1024]{1,0:T(8,128)(2,1)}, u32[]{:S(2)}) copy-start(bf16[16,1024]{1,0:T(8,128)(2,1)} %param.6) | copy-start | bytes 98308
  6.1 114.8 %all-to-all-start = ((bf16[32,2,64,256]{3,2,1,0:T(8,128)(2,1)}), bf16[32,2,64,256]{3,2,1,0:T(8,128)(2,1)}, u32[]{:S(2)}, u32[]{:S(2)}) async-start(bf16[32,2,64,256]{3,2,1,0:T(8,128)(2,1)} %bitcast.5), calls=%async_computation | async-start | bytes 4194304 | tf_op jit(solution)/shard_map/all_to_all | solution.py:82
  21.7 14.3 %collective-permute-start = (bf16[16,1024]{1,0:T(8,128)(2,1)S(1)}, bf16[16,1024]{1,0:T(8,128)(2,1)S(1)}, u32[]{:S(2)}, u32[]{:S(2)}) collective-permute-start(bf16[16,1024]{1,0:T(8,128)(2,1)S(1)} %copy-done.2), channel_id=1, source_target_pairs={{0,1},{1,0},{2,3},{3,2},{4,5},{5,4},{6,7},{7,6},{8,9},{9,8},{10,11... | collective-permute-start | bytes 98312 | tf_op jit(solution)/shard_map/ppermute | solution.py:18
  125.2 3.5 %copy-start.1 = (f32[256,4096]{1,0:T(8,128)S(1)}, f32[256,4096]{1,0:T(8,128)}, u32[]{:S(2)}) copy-start(f32[256,4096]{1,0:T(8,128)} %get-tuple-element.15) | copy-start | bytes 12582916
  131.2 12.7 %collective-permute-start.3 = (f32[16,8]{1,0:T(8,128)S(1)}, f32[16,8]{1,0:T(8,128)S(1)}, u32[]{:S(2)}, u32[]{:S(2)}) collective-permute-start(f32[16,8]{1,0:T(8,128)S(1)} %slice_select_fusion.1), channel_id=1, source_target_pairs={{0,1},{1,0},{2,3},{3,2},{4,5},{5,4},{6,7},{7,6},{8,9},{9,8},{10,11... | collective-permute-start | bytes 1544 | tf_op jit(solution)/shard_map/ppermute | solution.py:18
  134.7 9.2 %collective-permute-start.1 = (f32[16,8]{1,0:T(8,128)S(1)}, f32[16,8]{1,0:T(8,128)S(1)}, u32[]{:S(2)}, u32[]{:S(2)}) collective-permute-start(f32[16,8]{1,0:T(8,128)S(1)} %slice_select_fusion.2), channel_id=1, source_target_pairs={{0,1},{1,0},{2,3},{3,2},{4,5},{5,4},{6,7},{7,6},{8,9},{9,8},{10,11... | collective-permute-start | bytes 1544 | tf_op jit(solution)/shard_map/ppermute | solution.py:18
  140.4 6.2 %collective-permute-start.2 = (f32[16,8,128]{2,1,0:T(8,128)S(1)}, f32[16,8,128]{2,1,0:T(8,128)S(1)}, u32[]{:S(2)}, u32[]{:S(2)}) collective-permute-start(f32[16,8,128]{2,1,0:T(8,128)S(1)} %slice_select_fusion), channel_id=1, source_target_pairs={{0,1},{1,0},{2,3},{3,2},{4,5},{5,4},{6,7},{7,6},{8,9},{9,8},{10,11... | collective-permute-start | bytes 196616 | tf_op jit(solution)/shard_map/ppermute | solution.py:18
where the time goes:
time: 149 us; the launch traced here: 147 us
  waiting for transfers between devices  80.4 us (54%)
  starting transfers between devices  28.2 us (19%)
  local copies, waits for them, and re-layouts  14 us (9%)
  matrix products  13.7 us (9%)
  other arithmetic  10.1 us (7%)
    all_to_all x1, waiting for transfers between devices, on_device(): lax.all_to_all(outgoing, 'batch', split_axis=0, concat_axis=0, tiled=True)  77.7 us
    all_to_all x1, starting transfers between devices, on_device(): lax.all_to_all(outgoing, 'batch', split_axis=0, concat_axis=0, tiled=True)  15.6 us
    ppermute x4, starting transfers between devices, swapped(): return lax.ppermute(value, axis, pairs)  12.6 us
    reduce_sum x2, other arithmetic, partial_softmax(): total = jnp.sum(weights, axis=-1)  6.53 us
    reshape x1, local copies, waits for them, and re-layouts, on_device(): keep_suffix = keep_suffix.reshape(vec_rows, n_batch * capacity * half)  6.15 us
    dot_general x2, matrix products, partial_softmax(): jnp.dot(weights.astype(jnp.bfloat16), values, preferred_element_type=jnp....  5.72 us
    dot_general x1, matrix products, on_device(): jnp.einsum('qd,td->qt', vectors, flat[:, :HD], preferred_element_type=jnp...  4.12 us
    dot_general x1, matrix products, on_device(): jnp.einsum('qd,td->qt', vectors, prompt_rows[:, :HD], preferred_element_t...  3.9 us
  transfers between devices with their start and end apart: 5, of which 2 were waited for; matrix products, arithmetic and copies ran while one was open for 14% of the time, Pallas kernels for 0%

commit v1 on v0

v1 whole, which is shorter than its diff:
```python
import functools
import math

import jax
import jax.numpy as jnp
from jax import lax
from jax.experimental import pallas as pl
from jax.experimental.pallas import tpu as pltpu
from jax.sharding import PartitionSpec as P

MESH = pl.DeviceIdType.MESH
F32 = jnp.float32
BF16 = jnp.bfloat16

HD = 128
BEAMS = 16
HEADS = 8
NZ = 16
UP = 8
DOWN = 7
SLOTS = 16
HALF = 64
CHUNK = 512
MSG = 144
BIG = -1.0e30
EXPO = HD**-0.5 * math.log2(math.e)

ASK = {1: 0, 2: 1, 3: 2, 4: 3, 5: 0, 6: 5, 7: 6, 8: 7}
BACK = {1: 0, 2: 1, 3: 0, 4: 3, 5: 0, 6: 5, 7: 0, 8: 7}


def slot_of(sign, distance):
    return distance if sign > 0 else UP + distance


def place_of(slot):
    return (1, slot) if slot <= UP else (-1, slot - UP)


def children(table, slot):
    if slot == 0:
        return [s for s in range(1, SLOTS) if table[place_of(s)[1]] == 0]
    sign, distance = place_of(slot)
    return [s for s in range(1, SLOTS) if place_of(s)[0] == sign and table[place_of(s)[1]] == distance]


def iota(shape, dim):
    return lax.broadcasted_iota(jnp.int32, shape, dim)


def split3(value):
    first = value.astype(BF16).astype(F32)
    rest = value - first
    second = rest.astype(BF16).astype(F32)
    return (first, second, rest - second)


def pack(ref, slot, acc, top, total):
    row = iota((16, HD), 0)
    extra = jnp.zeros((16, HD), F32)
    for i, part in enumerate(split3(top) + split3(total)):
        extra = jnp.where(row == i, part, extra)
    ref[slot, 0:HD] = acc.astype(BF16)
    ref[slot, HD:MSG] = extra.astype(BF16)


def unpack(ref, slot):
    extra = ref[slot, HD:MSG].astype(F32)
    top = extra[0:1] + extra[1:2] + extra[2:3]
    total = extra[3:4] + extra[4:5] + extra[5:6]
    return (ref[slot, 0:HD].astype(F32), top, total)


def combine(a, b):
    top = jnp.maximum(a[1], b[1])
    scale_a = jnp.exp2((a[1] - top) * EXPO)
    scale_b = jnp.exp2((b[1] - top) * EXPO)
    return (a[0] * scale_a + b[0] * scale_b, top, a[2] * scale_a + b[2] * scale_b)


def attend(keys, values, vectors, keep):
    scores = jnp.where(keep, jnp.dot(keys, vectors, preferred_element_type=F32), BIG)
    top = jnp.max(scores, axis=0, keepdims=True)
    weights = jnp.where(keep, jnp.exp2((scores - top) * EXPO), 0.0)
    total = jnp.sum(weights, axis=0, keepdims=True)
    acc = lax.dot_general(
        values, weights.astype(BF16), (((0,), (0,)), ((), ())), preferred_element_type=F32
    )
    return (acc, top, total)


def kernel(
    length_ref, q_hbm, prompt_hbm, pool_hbm, table_hbm, parents_hbm, out_ref,
    q_v, prompt_v, pool_v, table_v, parents_v, sel_v, sel_s, keep_v,
    ask_own, ask_pair, part, part_out, part_in, sum_out, sum_in, run_acc, run_row,
    local_sem, prompt_sem, mate_sem, ask_ss, ask_rs, askx_ss, askx_rs, partx_ss, partx_rs, sum_ss, sum_rs,
):
    batch = lax.axis_index("batch")
    mp = lax.axis_index("mp")
    z = batch // 2
    core = batch % 2
    half = mp % 2
    pair = (batch, mp + 1 - 2 * half)
    mate = (batch + 1 - 2 * core, mp)

    def along(offset):
        return ((batch + 2 * (offset % NZ)) % (2 * NZ), mp)

    own_pool = pool_v.at[pl.ds(core * 32, 32)]
    loads = [
        pltpu.make_async_copy(q_hbm, q_v, local_sem.at[0]),
        pltpu.make_async_copy(table_hbm, table_v, local_sem.at[1]),
        pltpu.make_async_copy(parents_hbm, parents_v, local_sem.at[2]),
        pltpu.make_async_copy(pool_hbm, own_pool, local_sem.at[3]),
    ]
    for copy in loads:
        copy.start()
    n_prompt = prompt_v.shape[0] // 1024
    prompt_loads = []
    for i in range(n_prompt):
        rows = pl.ds(i * 1024, 1024)
        prompt_loads.append(
            pltpu.make_async_copy(prompt_hbm.at[rows], prompt_v.at[rows], prompt_sem.at[i])
        )
        prompt_loads[-1].start()

    offsets = set()
    for s in range(1, SLOTS):
        sign, d = place_of(s)
        for table in (ASK, BACK):
            offsets.add(sign * (d - table[d]))
            offsets.add(-sign * (d - table[d]))
    peers = [pair, mate] + [along(o) for o in sorted(offsets)]
    barrier = pltpu.get_barrier_semaphore()
    for peer in peers:
        pl.semaphore_signal(barrier, inc=1, device_id=peer, device_id_type=MESH)

    loads[0].wait()
    stacked = jnp.concatenate([q_v[:, h * HD : (h + 1) * HD] for h in range(HEADS)], axis=0)
    ask_own[0] = stacked.astype(F32).T.astype(BF16)
    pl.semaphore_wait(barrier, len(peers))

    def remote(src, dst, send, recv, device):
        return pltpu.make_async_remote_copy(
            src_ref=src, dst_ref=dst, send_sem=send, recv_sem=recv, device_id=device, device_id_type=MESH
        )

    def ask(slot):
        sign, d = place_of(slot)
        source = 0 if ASK[d] == 0 else slot_of(sign, ASK[d])
        return remote(
            ask_own.at[source], ask_own.at[slot], ask_ss.at[slot], ask_rs.at[slot], along(sign * (d - ASK[d]))
        )

    def askx(slot):
        return remote(ask_own.at[slot], ask_pair.at[slot], askx_ss.at[slot], askx_rs.at[slot], pair)

    def partx(slot):
        return remote(part_out.at[slot], part_in.at[slot], partx_ss.at[slot], partx_rs.at[slot], pair)

    def back(slot):
        sign, d = place_of(slot)
        return remote(
            sum_out.at[slot], sum_in.at[slot], sum_ss.at[slot], sum_rs.at[slot], along(-sign * (d - BACK[d]))
        )

    to_mate = remote(pool_hbm, own_pool, mate_sem.at[0], mate_sem.at[1], mate)

    def hand_on(slot):
        if slot:
            ask(slot).wait_recv()
        for child in sorted(children(ASK, slot), key=lambda s: -place_of(s)[1]):
            ask(child).start()
        askx(slot).start()

    def choose():
        loads[1].wait()
        loads[2].wait()
        n = parents_v.shape[1]
        entry = table_v[...]
        local = jnp.where(entry // 64 == z, entry % 64, -1).astype(F32).astype(BF16)
        picked = jnp.where(parents_v[...] == iota((n, n), 0), 1.0, 0.0).astype(BF16)
        named = jnp.dot(local, picked, preferred_element_type=F32)
        block = iota((64, n), 0).astype(F32)
        hit = jnp.zeros((64, n), F32)
        for j in range(4):
            hit = jnp.where(named[j : j + 1] == block, 1.0, hit)
        group = jnp.where(iota((n, 128), 0) // BEAMS == iota((n, 128), 1), 1.0, 0.0).astype(BF16)
        count = jnp.dot(hit.astype(BF16), group, preferred_element_type=F32)
        number = iota((32, 128), 0)
        row = iota((8, 128), 0)
        chosen = jnp.zeros((8, 128), jnp.int32)
        for owner in range(2):
            got = count[owner * 32 : owner * 32 + 32] > 0.5
            low = jnp.min(jnp.where(got, number, 32), axis=0, keepdims=True)
            low = jnp.where(low > 31, 0, low) + owner * 32
            high = jnp.max(jnp.where(got, number, 0), axis=0, keepdims=True) + owner * 32
            chosen = jnp.where(row == 2 * owner, low, chosen)
            chosen = jnp.where(row == 2 * owner + 1, high, chosen)
        sel_v[...] = chosen
        to_smem = pltpu.make_async_copy(sel_v, sel_s, local_sem.at[4])
        to_smem.start()
        spread = jnp.where(iota((128, n), 1) // BEAMS == iota((128, n), 0), 1.0, 0.0).astype(BF16)
        wide = jnp.dot(chosen.astype(F32).astype(BF16), spread, preferred_element_type=F32)
        uses = jnp.zeros((8, n), F32)
        for j in range(4):
            uses = jnp.where(named[j : j + 1] == wide, 1.0, uses)
        twin = jnp.concatenate([wide[0:1] - 1.0, wide[0:1], wide[2:3] - 1.0, wide[2:3], wide[4:8]], axis=0)
        wide_row = iota((8, n), 0)
        uses = jnp.where((wide == twin) | (wide_row > 3), 0.0, uses)
        tiled = jnp.concatenate([uses] * NZ, axis=0)
        own = iota((8 * NZ, n), 1) // BEAMS == 2 * (iota((8 * NZ, n), 0) // 8) + core
        tile = jnp.where(iota((n, 256), 0) % BEAMS == iota((n, 256), 1) % BEAMS, 1.0, 0.0).astype(BF16)
        rows = jnp.where(own, tiled, 0.0).astype(BF16)
        keep_v[...] = jnp.dot(rows, tile, preferred_element_type=F32)
        to_smem.wait()

    def vectors(slot):
        return jnp.concatenate([ask_own[slot], ask_pair[slot]], axis=1)

    def suffix(slot):
        sign, d = place_of(slot)
        where = (z - sign * d + NZ) % NZ
        request = 2 * where + core
        blocks = [pool_v[sel_s[k, request]] for k in range(4)]
        keys = jnp.concatenate([b[:, :HD] for b in blocks], axis=0)
        values = jnp.concatenate([b[:, HD:] for b in blocks], axis=0)
        rows = keep_v[pl.ds(pl.multiple_of(where * 8, 8), 8), :]
        keep = jnp.concatenate([jnp.broadcast_to(rows[k : k + 1], (HALF, 256)) for k in range(4)], axis=0)
        return attend(keys, values, vectors(slot), keep > 0.5)

    def give(slot, result):
        acc, top, total = result
        part[slot, 0:HD] = acc[:, :HD]
        part[slot, HD : HD + 1] = top[:, :HD]
        part[slot, HD + 1 : HD + 2] = total[:, :HD]
        pack(part_out, slot, acc[:, HD:], top[:, HD:], total[:, HD:])
        partx(slot).start()

    def work(slot):
        askx(slot).wait_recv()
        give(slot, suffix(slot))

    def own_part(slot):
        return (part[slot, 0:HD], part[slot, HD : HD + 1], part[slot, HD + 1 : HD + 2])

    def merge(slot):
        partx(slot).wait_recv()
        result = combine(own_part(slot), unpack(part_in, slot))
        for child in children(BACK, slot):
            back(child).wait_recv()
            result = combine(result, unpack(sum_in, child))
        pack(sum_out, slot, *result)
        back(slot).start()

    def prompt(first, last):
        query = vectors(0)

        def step(i, carry):
            start = pl.multiple_of(i * CHUNK, CHUNK)
            rows = prompt_v[pl.ds(start, CHUNK), :]
            token = start + iota((CHUNK, 256), 0)
            position = token // HALF * (2 * HALF) + half * HALF + token % HALF
            keep = position < length_ref[0]
            result = attend(rows[:, :HD], rows[:, HD:], query, keep)
            acc, top, total = combine((run_acc[...], run_row[0:1], run_row[1:2]), result)
            run_acc[...] = acc
            run_row[0:1] = top
            run_row[1:2] = total
            return carry

        lax.fori_loop(first, last, step, 0)

    def both(*distances):
        return [slot_of(sign, d) for d in distances for sign in (1, -1) if sign > 0 or d <= DOWN]

    hand_on(0)
    to_mate.start()
    run_acc[...] = jnp.zeros_like(run_acc)
    run_row[0:1] = jnp.full((1, 256), BIG, F32)
    run_row[1:2] = jnp.zeros((1, 256), F32)
    choose()
    for s in both(1):
        hand_on(s)
    askx(0).wait_recv()
    for copy in prompt_loads:
        copy.wait()
    prompt(0, 4)
    for s in both(5, 2):
        hand_on(s)
    loads[3].wait()
    to_mate.wait()
    for s in both(1):
        work(s)
    prompt(4, 6)
    for s in both(6, 3):
        hand_on(s)
    for s in both(5, 2):
        work(s)
    for s in both(7, 4):
        hand_on(s)
    for s in both(6, 3):
        work(s)
    for s in both(5, 2):
        if s in both(2):
            merge(s)
    for s in both(8):
        hand_on(s)
    for s in both(7, 4):
        work(s)
    for s in both(6):
        merge(s)
    for s in both(1):
        merge(s)
    for s in both(8):
        work(s)
    for s in both(4):
        merge(s)
    for s in both(5):
        merge(s)
    prompt(6, 8)
    give(0, combine((run_acc[...], run_row[0:1], run_row[1:2]), suffix(0)))
    for s in both(8, 3, 7):
        merge(s)
    partx(0).wait_recv()
    result = combine(own_part(0), unpack(part_in, 0))
    for s in both(1, 5, 3, 7):
        back(s).wait_recv()
        result = combine(result, unpack(sum_in, s))
    final = (result[0] / result[2]).T
    for h in range(HEADS):
        out_ref[:, h * HD : (h + 1) * HD] = final[h * BEAMS : (h + 1) * BEAMS, :]
    for s in range(SLOTS):
        askx(s).wait_send()
        partx(s).wait_send()
        if s:
            ask(s).wait_send()
            back(s).wait_send()


def on_device(queries, prompt_cache, pool, block_table, parents, lengths):
    rows = block_table.shape[0]
    any_space = pl.BlockSpec(memory_space=pl.ANY)
    dma = pltpu.SemaphoreType.DMA
    return pl.pallas_call(
        kernel,
        out_shape=jax.ShapeDtypeStruct((BEAMS, HEADS * HD), F32),
        in_specs=[pl.BlockSpec(memory_space=pltpu.SMEM)] + [any_space] * 5,
        out_specs=pl.BlockSpec(memory_space=pltpu.VMEM),
        scratch_shapes=[
            pltpu.VMEM((BEAMS, HEADS * HD), BF16),
            pltpu.VMEM((4096, 2 * HD), BF16),
            pltpu.VMEM((64, HALF, 2 * HD), BF16),
            pltpu.VMEM((4, rows), jnp.int32),
            pltpu.VMEM((1, rows), jnp.int32),
            pltpu.VMEM((8, 128), jnp.int32),
            pltpu.SMEM((8, 128), jnp.int32),
            pltpu.VMEM((8 * NZ, 256), F32),
            pltpu.VMEM((SLOTS, HD, HD), BF16),
            pltpu.VMEM((SLOTS, HD, HD), BF16),
            pltpu.VMEM((SLOTS, HD + 8, HD), F32),
            pltpu.VMEM((SLOTS, MSG, HD), BF16),
            pltpu.VMEM((SLOTS, MSG, HD), BF16),
            pltpu.VMEM((SLOTS, MSG, HD), BF16),
            pltpu.VMEM((SLOTS, MSG, HD), BF16),
            pltpu.VMEM((HD, 256), F32),
            pltpu.VMEM((8, 256), F32),
            dma((5,)),
            dma((4,)),
            dma((2,)),
        ]
        + [dma((SLOTS,))] * 8,
        compiler_params=pltpu.CompilerParams(
            collective_id=0, has_side_effects=True, vmem_limit_bytes=48 * 1024 * 1024
        ),
        name="carried_queries",
    )(
        lengths,
        queries,
        prompt_cache[0, 0],
        pool[:, 0],
        block_table.T,
        parents.reshape(1, rows),
    )


def solution(mesh):
    return jax.shard_map(
        on_device,
        mesh=mesh,
        in_specs=(
            P("batch", "mp"),
            P("batch", "mp", None, None),
            P("batch", "mp", None, None),
            P(),
            P(),
            P("batch"),
        ),
        out_specs=P("batch", "mp"),
        check_vma=False,
    )
```

time: 149 us -> 69 us (0.46)
  waiting for transfers between devices: 80.4 us -> 0 us
  Pallas kernels: 0 us -> 62.1 us
  starting transfers between devices: 28.2 us -> 0 us
  matrix products: 13.7 us -> 0 us
  other arithmetic: 10.1 us -> 0 us
  local copies, waits for them, and re-layouts: 14 us -> 5.58 us
    all_to_all x1 -> x0, waiting for transfers between devices: 77.7 us -> none  [on_device(): lax.all_to_all(outgoing, 'batch', split_axis=0, concat_axis=0, tiled=True)]
    pallas_call x0 -> x1, Pallas kernels: none -> 62.1 us  [on_device(): pl.pallas_call(kernel, out_shape=jax.ShapeDtypeStruct((BEAMS, HEADS * HD)...]
    all_to_all x1 -> x0, starting transfers between devices: 15.6 us -> none  [on_device(): lax.all_to_all(outgoing, 'batch', split_axis=0, concat_axis=0, tiled=True)]
    dot_general x4 -> x0, matrix products: 13.7 us -> none  [the longest x2 5.72 us: partial_softmax(): jnp.dot(weights.astype(jnp.bfloat16), values, preferred_element_type=jnp....]
    ppermute x4 -> x0, starting transfers between devices: 12.6 us -> none  [swapped(): return lax.ppermute(value, axis, pairs)]
    reduce_sum x4 -> x0, other arithmetic: 6.77 us -> none  [the longest x2 6.53 us: partial_softmax(): total = jnp.sum(weights, axis=-1)]
    reshape x2 -> x0, local copies, waits for them, and re-layouts: 6.24 us -> none  [the longest x1 6.15 us: on_device(): keep_suffix = keep_suffix.reshape(vec_rows, n_batch * capacity * half)]
    unnamed x10 -> x11, local copies, waits for them, and re-layouts: 1.61 us -> 5.58 us
  transfers between devices with their start and end apart: 5 -> 0, of which waited for: 2 -> 0; matrix products, arithmetic and copies ran while one was open for 14% -> 0% of each run, Pallas kernels for 0% -> 0%
where the time goes in v1:
time: 69 us; the launch traced here: 68.3 us
  Pallas kernels  62.1 us (90%)
  local copies, waits for them, and re-layouts  5.58 us (8%)
    pallas_call x1, Pallas kernels, on_device(): pl.pallas_call(kernel, out_shape=jax.ShapeDtypeStruct((BEAMS, HEADS * HD)...  62.1 us
    unnamed x11, local copies, waits for them, and re-layouts  5.58 us

profile of v1, /device:TPU:24, one launch (start us, length us, event | category | flops | bytes accessed | tf_op | source)
XLA Modules:
  0.0 68.3 jit_solution(8370379204432210414)
XLA Ops:
  0.7 0.0 copy-start
  0.7 1.6 %copy-done = bf16[1,1,4096,256]{3,2,1,0:T(8,128)(2,1)S(1)} copy-done((bf16[1,1,4096,256]{3,2,1,0:T(8,128)(2,1)S(1)}, bf16[1,1,4096,256]{3,2,1,0:T(8,128)(2,1)}, u32[]{:S(2)}) %copy-start) | copy-done | bytes 2097176
  2.2 0.0 copy-start.1
  2.2 1.2 %copy-done.1 = bf16[32,1,64,256]{3,2,1,0:T(8,128)(2,1)S(1)} copy-done((bf16[32,1,64,256]{3,2,1,0:T(8,128)(2,1)S(1)}, bf16[32,1,64,256]{3,2,1,0:T(8,128)(2,1)}, u32[]{:S(2)}) %copy-start.1) | copy-done | bytes 1048600
  3.5 0.0 copy-start.2
  3.5 0.8 %copy-done.2 = bf16[16,1024]{1,0:T(8,128)(2,1)S(1)} copy-done((bf16[16,1024]{1,0:T(8,128)(2,1)S(1)}, bf16[16,1024]{1,0:T(8,128)(2,1)}, u32[]{:S(2)}) %copy-start.2) | copy-done | bytes 32792
  4.2 0.0 copy-start.3
  4.2 0.7 %copy-done.3 = s32[512,4]{0,1:T(4,128)S(1)} copy-done((s32[512,4]{0,1:T(4,128)S(1)}, s32[512,4]{0,1:T(4,128)}, u32[]{:S(2)}) %copy-start.3) | copy-done | bytes 8216
  4.9 0.0 copy-start.4
  4.9 0.7 copy-done.4
  5.6 62.1 %carried_queries.1 = f32[16,1024]{1,0:T(8,128)S(1)} custom-call(s32[1]{0:T(128)S(6)} %copy.8.length_ref, bf16[16,1024]{1,0:T(8,128)(2,1)S(1)} %copy-done.2, bf16[4096,256]{1,0:T(8,128)(2,1)S(1)} %bitcast.4, bf16[32,64,256]{2,1,0:T(8,128)(2,1)S(1)} %bitcast.5, s32[4,512]{1,0:T(4,128)S(1)} %bitcast.6, s32[1,512]{1,0:T(1,128)S(1)} %bitcast.7), custom_call_target="tpu_custom_call" | custom-call | tf_op jit(solution)/shard_map/carried_queries/pallas_call | solution.py:345
  67.7 0.6 copy.9
Async XLA Ops:
  0.7 1.6 %copy-start = (bf16[1,1,4096,256]{3,2,1,0:T(8,128)(2,1)S(1)}, bf16[1,1,4096,256]{3,2,1,0:T(8,128)(2,1)}, u32[]{:S(2)}) copy-start(bf16[1,1,4096,256]{3,2,1,0:T(8,128)(2,1)} %param.7) | copy-start | bytes 6291460
  2.2 1.2 %copy-start.1 = (bf16[32,1,64,256]{3,2,1,0:T(8,128)(2,1)S(1)}, bf16[32,1,64,256]{3,2,1,0:T(8,128)(2,1)}, u32[]{:S(2)}) copy-start(bf16[32,1,64,256]{3,2,1,0:T(8,128)(2,1)} %param.8) | copy-start | bytes 3145732
  3.5 0.8 %copy-start.2 = (bf16[16,1024]{1,0:T(8,128)(2,1)S(1)}, bf16[16,1024]{1,0:T(8,128)(2,1)}, u32[]{:S(2)}) copy-start(bf16[16,1024]{1,0:T(8,128)(2,1)} %q_hbm.1) | copy-start | bytes 98308
  4.2 0.7 %copy-start.3 = (s32[512,4]{0,1:T(4,128)S(1)}, s32[512,4]{0,1:T(4,128)}, u32[]{:S(2)}) copy-start(s32[512,4]{0,1:T(4,128)} %param.9) | copy-start | bytes 24580
  4.9 0.7 copy-start.4

commit v2 on v1

v2 whole, which is shorter than its diff:
```python
import functools
import math

import jax
import jax.numpy as jnp
from jax import lax
from jax.experimental import pallas as pl
from jax.experimental.pallas import tpu as pltpu
from jax.sharding import PartitionSpec as P

MESH = pl.DeviceIdType.MESH
F32 = jnp.float32
BF16 = jnp.bfloat16

HD = 128
BEAMS = 16
HEADS = 8
NZ = 16
UP = 8
DOWN = 7
SLOTS = 16
HALF = 64
CHUNK = 512
MSG = 144
BIG = -1.0e30
EXPO = HD**-0.5 * math.log2(math.e)
OWN, OTHER = slice(0, HD), slice(HD, 2 * HD)

ASK = {1: 0, 2: 1, 3: 2, 4: 3, 5: 0, 6: 5, 7: 6, 8: 7}
BACK = {1: 0, 2: 1, 3: 0, 4: 3, 5: 0, 6: 5, 7: 0, 8: 7}
ASK_WIDE = ()
BACK_WIDE = (2, 4, 6, 8)
ORDER = (
    ("h", 0), ("c", 0), ("p", 0), ("p", 1), ("p", 2), ("p", 3), ("p", 4), ("w", 0), ("p", 5), ("p", 6),
    ("h", 1), ("h", 9), ("p", 7), ("p", 8), ("p", 9), ("p", 10), ("p", 11), ("a", 0), ("h", 5), ("h", 13),
    ("p", 12), ("h", 2), ("h", 10), ("w", 1), ("a", 1), ("w", 9), ("a", 9), ("p", 13), ("p", 14), ("p", 15),
    ("o", 0), ("w", 5), ("h", 6), ("h", 14), ("a", 5), ("w", 13), ("h", 3), ("h", 11), ("a", 13), ("w", 2),
    ("a", 2), ("w", 10), ("o", 2), ("a", 10), ("o", 10), ("h", 7), ("h", 15), ("w", 6), ("a", 6), ("h", 4),
    ("h", 12), ("w", 14), ("o", 6), ("a", 14), ("w", 3), ("o", 14), ("a", 3), ("w", 11), ("a", 11), ("o", 1),
    ("w", 7), ("a", 7), ("o", 9), ("w", 15), ("a", 15), ("h", 8), ("o", 15), ("w", 4), ("a", 4), ("o", 4),
    ("w", 12), ("a", 12), ("o", 5), ("o", 12), ("o", 13), ("m", 1), ("m", 9), ("w", 8), ("a", 8), ("o", 8),
    ("m", 15), ("m", 5), ("o", 3), ("m", 13), ("o", 11), ("o", 7), ("m", 3), ("m", 11), ("m", 7), ("m", 0),
)


LAST = (1, 9, 3, 11, 5, 13, 7, 15)


def slot_of(sign, distance):
    return distance if sign > 0 else UP + distance


def place_of(slot):
    return (1, slot) if slot <= UP else (-1, slot - UP)


def children(table, slot):
    if slot == 0:
        return [s for s in range(1, SLOTS) if table[place_of(s)[1]] == 0]
    sign, distance = place_of(slot)
    return [s for s in range(1, SLOTS) if place_of(s)[0] == sign and table[place_of(s)[1]] == distance]


def wide_ask(slot):
    return slot > 0 and place_of(slot)[1] in ASK_WIDE


def wide_back(slot):
    return slot > 0 and place_of(slot)[1] in BACK_WIDE


def iota(shape, dim):
    return lax.broadcasted_iota(jnp.int32, shape, dim)


def split3(value):
    first = value.astype(BF16).astype(F32)
    rest = value - first
    second = rest.astype(BF16).astype(F32)
    return (first, second, rest - second)


def pack(ref, result):
    acc, top, total = result
    row = iota((16, HD), 0)
    extra = jnp.zeros((16, HD), F32)
    for i, value in enumerate(split3(top) + split3(total)):
        extra = jnp.where(row == i, value, extra)
    ref[0:HD] = acc.astype(BF16)
    ref[HD:MSG] = extra.astype(BF16)


def unpack(ref):
    extra = ref[HD:MSG].astype(F32)
    top = extra[0:1] + extra[1:2] + extra[2:3]
    total = extra[3:4] + extra[4:5] + extra[5:6]
    return (ref[0:HD].astype(F32), top, total)


def combine(a, b):
    top = jnp.maximum(a[1], b[1])
    scale_a = jnp.exp2((a[1] - top) * EXPO)
    scale_b = jnp.exp2((b[1] - top) * EXPO)
    return (a[0] * scale_a + b[0] * scale_b, top, a[2] * scale_a + b[2] * scale_b)


def attend(keys, values, vectors, mask):
    scores = mask(jnp.dot(keys, vectors, preferred_element_type=F32))
    top = jnp.max(scores, axis=0, keepdims=True)
    weights = jnp.exp2((scores - top) * EXPO)
    total = jnp.sum(weights, axis=0, keepdims=True)
    acc = lax.dot_general(
        values, weights.astype(BF16), (((0,), (0,)), ((), ())), preferred_element_type=F32
    )
    return (acc, top, total)


def kernel(
    length_ref, q_hbm, prompt_hbm, pool_hbm, table_hbm, parents_hbm, out_ref,
    q_v, prompt_v, pool_v, table_v, parents_v, sel_v, sel_s, keep_v,
    ask_own, ask_pair, part, part_out, part_in, sum_out, sum_in, run,
    local_sem, prompt_sem, mate_sem, ask_ss, ask_rs, askw_ss, askw_rs, askx_ss, askx_rs, partx_ss, partx_rs, sum_ss, sum_rs,
):
    batch = lax.axis_index("batch")
    mp = lax.axis_index("mp")
    z = batch // 2
    core = batch % 2
    half = mp % 2
    pair = (batch, mp + 1 - 2 * half)
    mate = (batch + 1 - 2 * core, mp)

    def along(offset):
        return ((batch + 2 * (offset % NZ)) % (2 * NZ), mp)

    own_pool = pool_v.at[pl.ds(core * 32, 32)]
    loads = [
        pltpu.make_async_copy(q_hbm, q_v, local_sem.at[0]),
        pltpu.make_async_copy(table_hbm, table_v, local_sem.at[1]),
        pltpu.make_async_copy(parents_hbm, parents_v, local_sem.at[2]),
        pltpu.make_async_copy(pool_hbm, own_pool, local_sem.at[3]),
    ]
    for copy in loads:
        copy.start()
    n_prompt = prompt_v.shape[0] // 1024
    prompt_loads = []
    for i in range(n_prompt):
        rows = pl.ds(i * 1024, 1024)
        prompt_loads.append(
            pltpu.make_async_copy(prompt_hbm.at[rows], prompt_v.at[rows], prompt_sem.at[i])
        )
        prompt_loads[-1].start()

    offsets = set()
    for s in range(1, SLOTS):
        sign, d = place_of(s)
        for table in (ASK,):
            offsets.add(sign * (d - table[d]))
            offsets.add(-sign * (d - table[d]))
    peers = [pair, mate] + [along(o) for o in sorted(offsets)]
    barrier = pltpu.get_barrier_semaphore()
    for peer in peers:
        pl.semaphore_signal(barrier, inc=1, device_id=peer, device_id_type=MESH)

    loads[0].wait()
    stacked = jnp.concatenate([q_v[:, h * HD : (h + 1) * HD] for h in range(HEADS)], axis=0)
    ask_own[0] = stacked.astype(F32).T.astype(BF16)

    def remote(src, dst, send, recv, device):
        return pltpu.make_async_remote_copy(
            src_ref=src, dst_ref=dst, send_sem=send, recv_sem=recv, device_id=device, device_id_type=MESH
        )

    def came(table, slot):
        sign, d = place_of(slot)
        source = table[d]
        return (slot_of(sign, source) if source else 0, sign * (source - d))

    def ask(slot):
        source, offset = came(ASK, slot)
        return remote(ask_own.at[source], ask_own.at[slot], ask_ss.at[slot], ask_rs.at[slot], along(-offset))

    def askw(slot):
        source, offset = came(ASK, slot)
        return remote(ask_pair.at[source], ask_pair.at[slot], askw_ss.at[slot], askw_rs.at[slot], along(-offset))

    def askx(slot):
        return remote(ask_own.at[slot], ask_pair.at[slot], askx_ss.at[slot], askx_rs.at[slot], pair)

    def partx(slot):
        return remote(part_out.at[slot], part_in.at[slot], partx_ss.at[slot], partx_rs.at[slot], pair)

    def back(slot):
        _, offset = came(BACK, slot)
        sides = pl.ds(0, 2 if wide_back(slot) else 1)
        return remote(
            sum_out.at[slot, sides], sum_in.at[slot, sides], sum_ss.at[slot], sum_rs.at[slot], along(offset)
        )

    to_mate = remote(pool_hbm, own_pool, mate_sem.at[0], mate_sem.at[1], mate)

    def far_first(slots):
        return sorted(slots, key=lambda s: -place_of(s)[1])

    def hand_own(slot):
        if slot:
            ask(slot).wait_recv()
        for child in far_first(children(ASK, slot)):
            ask(child).start()
        if not wide_ask(slot):
            askx(slot).start()

    def hand_pair(slot):
        (askw if wide_ask(slot) else askx)(slot).wait_recv()
        for child in far_first(children(ASK, slot)):
            if wide_ask(child):
                askw(child).start()

    def choose():
        loads[1].wait()
        loads[2].wait()
        n = parents_v.shape[1]
        entry = table_v[...]
        local = jnp.where(entry // 64 == z, entry % 64, -1).astype(F32).astype(BF16)
        picked = jnp.where(parents_v[...] == iota((n, n), 0), 1.0, 0.0).astype(BF16)
        named = jnp.dot(local, picked, preferred_element_type=F32)
        block = iota((64, n), 0).astype(F32)
        hit = jnp.zeros((64, n), F32)
        for j in range(4):
            hit = jnp.where(named[j : j + 1] == block, 1.0, hit)
        group = jnp.where(iota((n, 128), 0) // BEAMS == iota((n, 128), 1), 1.0, 0.0).astype(BF16)
        count = jnp.dot(hit.astype(BF16), group, preferred_element_type=F32)
        number = iota((32, 128), 0)
        row = iota((8, 128), 0)
        chosen = jnp.zeros((8, 128), jnp.int32)
        for owner in range(2):
            got = count[owner * 32 : owner * 32 + 32] > 0.5
            low = jnp.min(jnp.where(got, number, 32), axis=0, keepdims=True)
            low = jnp.where(low > 31, 0, low) + owner * 32
            high = jnp.max(jnp.where(got, number, 0), axis=0, keepdims=True) + owner * 32
            chosen = jnp.where(row == 2 * owner, low, chosen)
            chosen = jnp.where(row == 2 * owner + 1, high, chosen)
        sel_v[...] = chosen
        to_smem = pltpu.make_async_copy(sel_v, sel_s, local_sem.at[4])
        to_smem.start()
        spread = jnp.where(iota((128, n), 1) // BEAMS == iota((128, n), 0), 1.0, 0.0).astype(BF16)
        wide = jnp.dot(chosen.astype(F32).astype(BF16), spread, preferred_element_type=F32)
        uses = jnp.zeros((8, n), F32)
        for j in range(4):
            uses = jnp.where(named[j : j + 1] == wide, 1.0, uses)
        twin = jnp.concatenate([wide[0:1] - 1.0, wide[0:1], wide[2:3] - 1.0, wide[2:3], wide[4:8]], axis=0)
        wide_row = iota((8, n), 0)
        uses = jnp.where((wide == twin) | (wide_row > 3), 0.0, uses)
        tiled = jnp.concatenate([uses] * NZ, axis=0)
        own = iota((8 * NZ, n), 1) // BEAMS == 2 * (iota((8 * NZ, n), 0) // 8) + core
        tile = jnp.where(iota((n, 256), 0) % BEAMS == iota((n, 256), 1) % BEAMS, 1.0, 0.0).astype(BF16)
        rows = jnp.where(own, tiled, 0.0).astype(BF16)
        keep_v[...] = jnp.where(jnp.dot(rows, tile, preferred_element_type=F32) > 0.5, 0.0, BIG)
        to_smem.wait()

    def vectors(slot):
        return jnp.concatenate([ask_own[slot], ask_pair[slot]], axis=1)

    def suffix(slot):
        sign, d = place_of(slot)
        where = (z - sign * d + NZ) % NZ
        request = 2 * where + core
        blocks = [pool_v[sel_s[k, request]] for k in range(4)]
        keys = jnp.concatenate([b[:, :HD] for b in blocks], axis=0)
        values = jnp.concatenate([b[:, HD:] for b in blocks], axis=0)
        rows = keep_v[pl.ds(pl.multiple_of(where * 8, 8), 8), :]

        def mask(scores):
            return jnp.concatenate(
                [scores[k * HALF : (k + 1) * HALF] + rows[k : k + 1] for k in range(4)], axis=0
            )

        return attend(keys, values, vectors(slot), mask)

    def keep_sums(slot, result):
        part[slot, 0:HD] = result[0]
        part[slot, HD : HD + 1] = result[1]
        part[slot, HD + 1 : HD + 2] = result[2]

    def kept_sums(slot, lanes):
        return (part[slot, 0:HD, lanes], part[slot, HD : HD + 1, lanes], part[slot, HD + 1 : HD + 2, lanes])

    def work(slot):
        result = suffix(slot)
        keep_sums(slot, result)

    def send_on(slot):
        own, other = kept_sums(slot, OWN), kept_sums(slot, OTHER)
        if slot == 0:
            own = combine(own, (run[0:HD, OWN], run[HD : HD + 1, OWN], run[HD + 1 : HD + 2, OWN]))
            other = combine(other, (run[0:HD, OTHER], run[HD : HD + 1, OTHER], run[HD + 1 : HD + 2, OTHER]))
        grown = slot == 0
        for child in children(BACK, slot):
            if wide_back(child):
                back(child).wait_recv()
                own = combine(own, unpack(sum_in.at[child, 0]))
                other = combine(other, unpack(sum_in.at[child, 1]))
                grown = True
        if wide_back(slot):
            pack(sum_out.at[slot, 0], own)
            pack(sum_out.at[slot, 1], other)
            back(slot).start()
        else:
            pack(part_out.at[slot], other)
            partx(slot).start()
            if grown:
                part[slot, 0:HD, OWN] = own[0]
                part[slot, HD : HD + 1, OWN] = own[1]
                part[slot, HD + 1 : HD + 2, OWN] = own[2]

    def merge(slot):
        partx(slot).wait_recv()
        result = combine(kept_sums(slot, OWN), unpack(part_in.at[slot]))
        for child in LAST if slot == 0 else children(BACK, slot):
            if not wide_back(child):
                back(child).wait_recv()
                result = combine(result, unpack(sum_in.at[child, 0]))
        if slot:
            pack(sum_out.at[slot, 0], result)
            back(slot).start()
        return result

    def prompt(i, side):
        lanes = slice(side * HD, (side + 1) * HD)
        start = pl.multiple_of(i * CHUNK, CHUNK)
        rows = prompt_v[pl.ds(start, CHUNK), :]
        inside = iota((HALF, HD), 0)

        def mask(scores):
            parts = []
            for k in range(CHUNK // HALF):
                room = length_ref[0] - 2 * start - (2 * k + half) * HALF
                parts.append(jnp.where(inside < room, scores[k * HALF : (k + 1) * HALF], BIG))
            return jnp.concatenate(parts, axis=0)

        result = attend(rows[:, :HD], rows[:, HD:], (ask_pair if side else ask_own)[0], mask)
        result = combine((run[0:HD, lanes], run[HD : HD + 1, lanes], run[HD + 1 : HD + 2, lanes]), result)
        run[0:HD, lanes] = result[0]
        run[HD : HD + 1, lanes] = result[1]
        run[HD + 1 : HD + 2, lanes] = result[2]

    run[...] = jnp.zeros_like(run)
    run[HD : HD + 1] = jnp.full((1, 256), BIG, F32)
    pl.semaphore_wait(barrier, len(peers))

    chunks = prompt_v.shape[0] // CHUNK
    loaded = set()
    for kind, s in ORDER:
        if kind == "h":
            hand_own(s)
            if s == 0:
                to_mate.start()
        elif kind == "w":
            hand_pair(s)
        elif kind == "c":
            choose()
        elif kind == "a":
            if "pool" not in loaded:
                loads[3].wait()
                to_mate.wait()
                loaded.add("pool")
            work(s)
        elif kind == "o":
            send_on(s)
        elif kind == "p":
            piece = s % chunks * CHUNK // 1024
            if piece not in loaded:
                prompt_loads[piece].wait()
                loaded.add(piece)
            prompt(s % chunks, s // chunks)
        elif kind == "m" and s:
            merge(s)
    result = merge(0)
    final = (result[0] / result[2]).T
    for h in range(HEADS):
        out_ref[:, h * HD : (h + 1) * HD] = final[h * BEAMS : (h + 1) * BEAMS, :]
    for s in range(SLOTS):
        if not wide_ask(s):
            askx(s).wait_send()
        if not wide_back(s):
            partx(s).wait_send()
        if s:
            ask(s).wait_send()
            back(s).wait_send()
            if wide_ask(s):
                askw(s).wait_send()


def on_device(queries, prompt_cache, pool, block_table, parents, lengths):
    rows = block_table.shape[0]
    any_space = pl.BlockSpec(memory_space=pl.ANY)
    dma = pltpu.SemaphoreType.DMA
    return pl.pallas_call(
        kernel,
        out_shape=jax.ShapeDtypeStruct((BEAMS, HEADS * HD), F32),
        in_specs=[pl.BlockSpec(memory_space=pltpu.SMEM)] + [any_space] * 5,
        out_specs=pl.BlockSpec(memory_space=pltpu.VMEM),
        scratch_shapes=[
            pltpu.VMEM((BEAMS, HEADS * HD), BF16),
            pltpu.VMEM((4096, 2 * HD), BF16),
            pltpu.VMEM((64, HALF, 2 * HD), BF16),
            pltpu.VMEM((4, rows), jnp.int32),
            pltpu.VMEM((1, rows), jnp.int32),
            pltpu.VMEM((8, 128), jnp.int32),
            pltpu.SMEM((8, 128), jnp.int32),
            pltpu.VMEM((8 * NZ, 256), F32),
            pltpu.VMEM((SLOTS, HD, HD), BF16),
            pltpu.VMEM((SLOTS, HD, HD), BF16),
            pltpu.VMEM((SLOTS, HD + 8, 2 * HD), F32),
            pltpu.VMEM((SLOTS, MSG, HD), BF16),
            pltpu.VMEM((SLOTS, MSG, HD), BF16),
            pltpu.VMEM((SLOTS, 2, MSG, HD), BF16),
            pltpu.VMEM((SLOTS, 2, MSG, HD), BF16),
            pltpu.VMEM((HD + 8, 2 * HD), F32),
            dma((5,)),
            dma((4,)),
            dma((2,)),
        ]
        + [dma((SLOTS,))] * 10,
        compiler_params=pltpu.CompilerParams(
            collective_id=0, has_side_effects=True, vmem_limit_bytes=60 * 1024 * 1024
        ),
        name="carried_queries",
    )(
        lengths,
        queries,
        prompt_cache[0, 0],
        pool[:, 0],
        block_table.T,
        parents.reshape(1, rows),
    )


def solution(mesh):
    return jax.shard_map(
        on_device,
        mesh=mesh,
        in_specs=(
            P("batch", "mp"),
            P("batch", "mp", None, None),
            P("batch", "mp", None, None),
            P(),
            P(),
            P("batch"),
        ),
        out_specs=P("batch", "mp"),
        check_vma=False,
    )
```

time: 69 us -> 58.1 us (0.84)
  Pallas kernels: 62.1 us -> 55.7 us
  local copies, waits for them, and re-layouts: 5.58 us -> 1.47 us
    pallas_call x1, Pallas kernels: 62.1 us -> 55.7 us  [on_device(): pl.pallas_call(kernel, out_shape=jax.ShapeDtypeStruct((BEAMS, HEADS * HD)...]
    unnamed x11 -> x1, local copies, waits for them, and re-layouts: 5.58 us -> 1.47 us
where the time goes in v2:
time: 58.1 us; the launch traced here: 57.9 us
  Pallas kernels  55.7 us (96%)
  local copies, waits for them, and re-layouts  1.47 us (3%)
  between operations  0.66 us (1%)
    pallas_call x1, Pallas kernels, on_device(): pl.pallas_call(kernel, out_shape=jax.ShapeDtypeStruct((BEAMS, HEADS * HD)...  55.7 us
    unnamed x1, local copies, waits for them, and re-layouts  1.47 us

profile of v2, /device:TPU:24, one launch (start us, length us, event | category | flops | bytes accessed | tf_op | source)
XLA Modules:
  0.0 57.9 jit_solution(11956037390598049214)
XLA Ops:
  0.7 55.7 %carried_queries.1 = f32[16,1024]{1,0:T(8,128)} custom-call(s32[1]{0:T(128)S(6)} %copy.8.length_ref, bf16[16,1024]{1,0:T(8,128)(2,1)} %q_hbm.1, bf16[4096,256]{1,0:T(8,128)(2,1)} %bitcast.4, bf16[32,64,256]{2,1,0:T(8,128)(2,1)} %bitcast.5, s32[4,512]{1,0:T(4,128)} %bitcast.6, s32[1,512]{1,0:T(1,128)} %bitcast.7), custom_call_target="tpu_custom_call" | custom-call | tf_op jit(solution)/shard_map/carried_queries/pallas_call | solution.py:397
  56.4 1.5 %copy.9 = f32[16,1024]{1,0:T(8,128)} copy(f32[16,1024]{1,0:T(8,128)} %carried_queries.1) | data formatting | bytes 131072

commit v3 on v2

--- a/solution.py
+++ b/solution.py
@@ -22,28 +22,30 @@
 HALF = 64
 CHUNK = 512
 MSG = 144
+EARLY = NZ // 2
 BIG = -1.0e30
 EXPO = HD**-0.5 * math.log2(math.e)
 OWN, OTHER = slice(0, HD), slice(HD, 2 * HD)
 
-ASK = {1: 0, 2: 1, 3: 2, 4: 3, 5: 0, 6: 5, 7: 6, 8: 7}
-BACK = {1: 0, 2: 1, 3: 0, 4: 3, 5: 0, 6: 5, 7: 0, 8: 7}
-ASK_WIDE = ()
-BACK_WIDE = (2, 4, 6, 8)
+ASK = {1: 0, 2: 4, 3: 1, 4: 5, 5: 0, 6: 4, 7: 5, 8: 5}
+BACK = {1: 2, 2: 0, 3: 2, 4: 2, 5: 6, 6: 0, 7: 6, 8: 6}
+ASK_WIDE = (3, 4)
+BACK_WIDE = (4, 7)
 ORDER = (
     ("h", 0), ("c", 0), ("p", 0), ("p", 1), ("p", 2), ("p", 3), ("p", 4), ("w", 0), ("p", 5), ("p", 6),
     ("h", 1), ("h", 9), ("p", 7), ("p", 8), ("p", 9), ("p", 10), ("p", 11), ("a", 0), ("h", 5), ("h", 13),
-    ("p", 12), ("h", 2), ("h", 10), ("w", 1), ("a", 1), ("w", 9), ("a", 9), ("p", 13), ("p", 14), ("p", 15),
-    ("o", 0), ("w", 5), ("h", 6), ("h", 14), ("a", 5), ("w", 13), ("h", 3), ("h", 11), ("a", 13), ("w", 2),
-    ("a", 2), ("w", 10), ("o", 2), ("a", 10), ("o", 10), ("h", 7), ("h", 15), ("w", 6), ("a", 6), ("h", 4),
-    ("h", 12), ("w", 14), ("o", 6), ("a", 14), ("w", 3), ("o", 14), ("a", 3), ("w", 11), ("a", 11), ("o", 1),
-    ("w", 7), ("a", 7), ("o", 9), ("w", 15), ("a", 15), ("h", 8), ("o", 15), ("w", 4), ("a", 4), ("o", 4),
-    ("w", 12), ("a", 12), ("o", 5), ("o", 12), ("o", 13), ("m", 1), ("m", 9), ("w", 8), ("a", 8), ("o", 8),
-    ("m", 15), ("m", 5), ("o", 3), ("m", 13), ("o", 11), ("o", 7), ("m", 3), ("m", 11), ("m", 7), ("m", 0),
+    ("p", 12), ("w", 1), ("a", 1), ("o", 1), ("h", 3), ("h", 11), ("w", 9), ("a", 9), ("o", 9), ("p", 13),
+    ("p", 14), ("p", 15), ("w", 5), ("h", 4), ("o", 0), ("a", 5), ("w", 13), ("o", 5), ("a", 13), ("h", 15),
+    ("h", 12), ("m", 1), ("o", 13), ("m", 9), ("w", 11), ("a", 11), ("o", 11), ("h", 7), ("w", 4), ("a", 4),
+    ("o", 4), ("h", 8), ("m", 5), ("w", 3), ("h", 2), ("a", 3), ("w", 15), ("o", 3), ("a", 15), ("w", 12),
+    ("m", 13), ("o", 15), ("a", 12), ("h", 14), ("m", 11), ("o", 12), ("w", 7), ("a", 7), ("o", 7), ("w", 8),
+    ("h", 6), ("a", 8), ("w", 2), ("h", 10), ("o", 8), ("a", 2), ("m", 3), ("o", 2), ("w", 14), ("a", 14),
+    ("o", 14), ("w", 6), ("a", 6), ("w", 10), ("o", 6), ("a", 10), ("m", 8), ("m", 2), ("m", 14), ("o", 10),
+    ("m", 6), ("m", 10),
 )
 
 
-LAST = (1, 9, 3, 11, 5, 13, 7, 15)
+LAST = (2, 10, 6, 14)
 
 
 def slot_of(sign, distance):
@@ -345,9 +347,18 @@
 
     run[...] = jnp.zeros_like(run)
     run[HD : HD + 1] = jnp.full((1, 256), BIG, F32)
+    chunks = prompt_v.shape[0] // CHUNK
+    early = z < EARLY
+
+    @pl.when(early)
+    def _():
+        choose()
+        for i, copy in enumerate(prompt_loads):
+            copy.wait()
+            for k in range(i * 1024 // CHUNK, (i + 1) * 1024 // CHUNK):
+                prompt(k, 0)
+
     pl.semaphore_wait(barrier, len(peers))
-
-    chunks = prompt_v.shape[0] // CHUNK
     loaded = set()
     for kind, s in ORDER:
         if kind == "h":
@@ -357,7 +368,7 @@
         elif kind == "w":
             hand_pair(s)
         elif kind == "c":
-            choose()
+            pl.when(~early)(choose)
         elif kind == "a":
             if "pool" not in loaded:
                 loads[3].wait()
@@ -368,10 +379,17 @@
             send_on(s)
         elif kind == "p":
             piece = s % chunks * CHUNK // 1024
-            if piece not in loaded:
-                prompt_loads[piece].wait()
+            if s < chunks:
+
+                @pl.when(~early)
+                def _():
+                    if piece not in loaded:
+                        prompt_loads[piece].wait()
+                    prompt(s, 0)
+
                 loaded.add(piece)
-            prompt(s % chunks, s // chunks)
+            else:
+                prompt(s - chunks, 1)
         elif kind == "m" and s:
             merge(s)
     result = merge(0)

time: 58.1 us -> 53.5 us (0.921)
  Pallas kernels: 55.7 us -> 51.2 us
    pallas_call x1, Pallas kernels: 55.7 us -> 51.2 us  [on_device(): pl.pallas_call(kernel, out_shape=jax.ShapeDtypeStruct((BEAMS, HEADS * HD)...]
where the time goes in v3:
time: 53.5 us; the launch traced here: 53.4 us
  Pallas kernels  51.2 us (96%)
  local copies, waits for them, and re-layouts  1.47 us (3%)
  between operations  0.66 us (1%)
    pallas_call x1, Pallas kernels, on_device(): pl.pallas_call(kernel, out_shape=jax.ShapeDtypeStruct((BEAMS, HEADS * HD)...  51.2 us
    unnamed x1, local copies, waits for them, and re-layouts  1.47 us

profile of v3, /device:TPU:24, one launch (start us, length us, event | category | flops | bytes accessed | tf_op | source)
XLA Modules:
  0.0 53.4 jit_solution(1198249494126139845)
XLA Ops:
  0.7 51.2 %carried_queries.1 = f32[16,1024]{1,0:T(8,128)} custom-call(s32[1]{0:T(128)S(6)} %copy.8.length_ref, bf16[16,1024]{1,0:T(8,128)(2,1)} %q_hbm.1, bf16[4096,256]{1,0:T(8,128)(2,1)} %bitcast.4, bf16[32,64,256]{2,1,0:T(8,128)(2,1)} %bitcast.5, s32[4,512]{1,0:T(4,128)} %bitcast.6, s32[1,512]{1,0:T(1,128)} %bitcast.7), custom_call_target="tpu_custom_call" | custom-call | tf_op jit(solution)/shard_map/carried_queries/pallas_call | solution.py:415
  51.9 1.5 %copy.9 = f32[16,1024]{1,0:T(8,128)} copy(f32[16,1024]{1,0:T(8,128)} %carried_queries.1) | data formatting | bytes 131072

commit v4 on v3

--- a/solution.py
+++ b/solution.py
@@ -414,7 +414,7 @@
     dma = pltpu.SemaphoreType.DMA
     return pl.pallas_call(
         kernel,
-        out_shape=jax.ShapeDtypeStruct((BEAMS, HEADS * HD), F32),
+        out_shape=pltpu.VMEM((BEAMS, HEADS * HD), F32),
         in_specs=[pl.BlockSpec(memory_space=pltpu.SMEM)] + [any_space] * 5,
         out_specs=pl.BlockSpec(memory_space=pltpu.VMEM),
         scratch_shapes=[
@@ -440,7 +440,7 @@
         ]
         + [dma((SLOTS,))] * 10,
         compiler_params=pltpu.CompilerParams(
-            collective_id=0, has_side_effects=True, vmem_limit_bytes=60 * 1024 * 1024
+            collective_id=0, has_side_effects=True, vmem_limit_bytes=54 * 1024 * 1024
         ),
         name="carried_queries",
     )(

time: 53.5 us -> 52 us (0.972)
  local copies, waits for them, and re-layouts: 1.47 us -> 0.63 us
  Pallas kernels: 51.2 us -> 50.6 us
    unnamed x1, local copies, waits for them, and re-layouts: 1.47 us -> 0.63 us
    pallas_call x1, Pallas kernels: 51.2 us -> 50.6 us  [on_device(): pl.pallas_call(kernel, out_shape=pltpu.VMEM((BEAMS, HEADS * HD), F32), in...]
where the time goes in v4:
time: 52 us; the launch traced here: 51.9 us
  Pallas kernels  50.6 us (97%)
  between operations  0.66 us (1%)
  local copies, waits for them, and re-layouts  0.63 us (1%)
    pallas_call x1, Pallas kernels, on_device(): pl.pallas_call(kernel, out_shape=pltpu.VMEM((BEAMS, HEADS * HD), F32), in...  50.6 us

profile of v4, /device:TPU:24, one launch (start us, length us, event | category | flops | bytes accessed | tf_op | source)
XLA Modules:
  0.0 51.9 jit_solution(8246938809089551775)
XLA Ops:
  0.7 50.6 %carried_queries.1 = f32[16,1024]{1,0:T(8,128)S(1)} custom-call(s32[1]{0:T(128)S(6)} %copy.9.length_ref, bf16[16,1024]{1,0:T(8,128)(2,1)} %q_hbm.1, bf16[4096,256]{1,0:T(8,128)(2,1)} %bitcast.4, bf16[32,64,256]{2,1,0:T(8,128)(2,1)} %bitcast.5, s32[4,512]{1,0:T(4,128)} %bitcast.6, s32[1,512]{1,0:T(1,128)} %bitcast.7), custom_call_target="tpu_custom_call" | custom-call | tf_op jit(solution)/shard_map/carried_queries/pallas_call | solution.py:415
  51.3 0.6 %copy.8 = f32[16,1024]{1,0:T(8,128)} copy(f32[16,1024]{1,0:T(8,128)S(1)} %carried_queries.1) | data formatting | bytes 131072

commit v5 on v4

--- a/solution.py
+++ b/solution.py
@@ -27,25 +27,24 @@
 EXPO = HD**-0.5 * math.log2(math.e)
 OWN, OTHER = slice(0, HD), slice(HD, 2 * HD)
 
-ASK = {1: 0, 2: 4, 3: 1, 4: 5, 5: 0, 6: 4, 7: 5, 8: 5}
-BACK = {1: 2, 2: 0, 3: 2, 4: 2, 5: 6, 6: 0, 7: 6, 8: 6}
-ASK_WIDE = (3, 4)
-BACK_WIDE = (4, 7)
+ASK = {1: 2, 2: 0, 3: 2, 4: 0, 5: 4, 6: 5, 7: 4, 8: 7}
+BACK = {1: 0, 2: 3, 3: 0, 4: 5, 5: 6, 6: 0, 7: 6, 8: 6}
+ASK_WIDE = (3, 6, 8)
+BACK_WIDE = (2, 4, 5, 7)
 ORDER = (
-    ("h", 0), ("c", 0), ("p", 0), ("p", 1), ("p", 2), ("p", 3), ("p", 4), ("w", 0), ("p", 5), ("p", 6),
-    ("h", 1), ("h", 9), ("p", 7), ("p", 8), ("p", 9), ("p", 10), ("p", 11), ("a", 0), ("h", 5), ("h", 13),
-    ("p", 12), ("w", 1), ("a", 1), ("o", 1), ("h", 3), ("h", 11), ("w", 9), ("a", 9), ("o", 9), ("p", 13),
-    ("p", 14), ("p", 15), ("w", 5), ("h", 4), ("o", 0), ("a", 5), ("w", 13), ("o", 5), ("a", 13), ("h", 15),
-    ("h", 12), ("m", 1), ("o", 13), ("m", 9), ("w", 11), ("a", 11), ("o", 11), ("h", 7), ("w", 4), ("a", 4),
-    ("o", 4), ("h", 8), ("m", 5), ("w", 3), ("h", 2), ("a", 3), ("w", 15), ("o", 3), ("a", 15), ("w", 12),
-    ("m", 13), ("o", 15), ("a", 12), ("h", 14), ("m", 11), ("o", 12), ("w", 7), ("a", 7), ("o", 7), ("w", 8),
-    ("h", 6), ("a", 8), ("w", 2), ("h", 10), ("o", 8), ("a", 2), ("m", 3), ("o", 2), ("w", 14), ("a", 14),
-    ("o", 14), ("w", 6), ("a", 6), ("w", 10), ("o", 6), ("a", 10), ("m", 8), ("m", 2), ("m", 14), ("o", 10),
-    ("m", 6), ("m", 10),
+    ("h", 0), ("c", 0), ("w", 0), ("p", 15), ("p", 10), ("p", 8), ("p", 9), ("h", 2), ("p", 1), ("h", 10),
+    ("h", 4), ("h", 12), ("p", 3), ("p", 12), ("p", 0), ("p", 5), ("h", 9), ("w", 2), ("p", 4), ("w", 10),
+    ("a", 2), ("h", 11), ("o", 2), ("h", 5), ("w", 4), ("w", 12), ("h", 3), ("a", 10), ("a", 4), ("h", 7),
+    ("a", 12), ("h", 13), ("o", 12), ("o", 4), ("w", 9), ("a", 9), ("h", 15), ("o", 9), ("w", 5), ("h", 1),
+    ("w", 3), ("o", 10), ("a", 0), ("a", 5), ("w", 7), ("a", 3), ("w", 13), ("w", 11), ("a", 13), ("a", 7),
+    ("p", 14), ("h", 8), ("w", 15), ("a", 15), ("o", 15), ("o", 13), ("o", 3), ("w", 1), ("w", 8), ("a", 8),
+    ("o", 8), ("o", 7), ("o", 5), ("a", 11), ("p", 13), ("o", 11), ("a", 1), ("h", 14), ("m", 9), ("w", 14),
+    ("a", 14), ("o", 1), ("p", 7), ("m", 8), ("h", 6), ("o", 14), ("m", 3), ("w", 6), ("a", 6), ("o", 6),
+    ("m", 11), ("m", 1), ("p", 2), ("p", 11), ("m", 14), ("p", 6), ("o", 0), ("m", 6),
 )
 
 
-LAST = (2, 10, 6, 14)
+LAST = (1, 9, 3, 11, 6, 14)
 
 
 def slot_of(sign, distance):
@@ -379,15 +378,11 @@
             send_on(s)
         elif kind == "p":
             piece = s % chunks * CHUNK // 1024
+            if piece not in loaded:
+                pl.when(~early)(prompt_loads[piece].wait)
+                loaded.add(piece)
             if s < chunks:
-
-                @pl.when(~early)
-                def _():
-                    if piece not in loaded:
-                        prompt_loads[piece].wait()
-                    prompt(s, 0)
-
-                loaded.add(piece)
+                pl.when(~early)(functools.partial(prompt, s, 0))
             else:
                 prompt(s - chunks, 1)
         elif kind == "m" and s:

time: 52 us -> 51.3 us (0.987)
  the two profiles are of different devices: /device:TPU:24 before, /device:TPU:44 now
where the time goes in v5:
time: 51.3 us; the launch traced here: 51.1 us
  Pallas kernels  49.9 us (97%)
  between operations  0.66 us (1%)
  local copies, waits for them, and re-layouts  0.63 us (1%)
    pallas_call x1, Pallas kernels, on_device(): pl.pallas_call(kernel, out_shape=pltpu.VMEM((BEAMS, HEADS * HD), F32), in...  49.9 us

profile of v5, /device:TPU:44, one launch (start us, length us, event | category | flops | bytes accessed | tf_op | source)
XLA Modules:
  0.0 51.1 jit_solution(3134183509283152231)
XLA Ops:
  0.7 49.9 %carried_queries.1 = f32[16,1024]{1,0:T(8,128)S(1)} custom-call(s32[1]{0:T(128)S(6)} %copy.9.length_ref, bf16[16,1024]{1,0:T(8,128)(2,1)} %q_hbm.1, bf16[4096,256]{1,0:T(8,128)(2,1)} %bitcast.4, bf16[32,64,256]{2,1,0:T(8,128)(2,1)} %bitcast.5, s32[4,512]{1,0:T(4,128)} %bitcast.6, s32[1,512]{1,0:T(1,128)} %bitcast.7), custom_call_target="tpu_custom_call" | custom-call | tf_op jit(solution)/shard_map/carried_queries/pallas_call | solution.py:410
  50.5 0.6 %copy.8 = f32[16,1024]{1,0:T(8,128)} copy(f32[16,1024]{1,0:T(8,128)S(1)} %carried_queries.1) | data formatting | bytes 131072

commit v6 on v5

--- a/solution.py
+++ b/solution.py
@@ -32,15 +32,15 @@
 ASK_WIDE = (3, 6, 8)
 BACK_WIDE = (2, 4, 5, 7)
 ORDER = (
-    ("h", 0), ("c", 0), ("w", 0), ("p", 15), ("p", 10), ("p", 8), ("p", 9), ("h", 2), ("p", 1), ("h", 10),
-    ("h", 4), ("h", 12), ("p", 3), ("p", 12), ("p", 0), ("p", 5), ("h", 9), ("w", 2), ("p", 4), ("w", 10),
-    ("a", 2), ("h", 11), ("o", 2), ("h", 5), ("w", 4), ("w", 12), ("h", 3), ("a", 10), ("a", 4), ("h", 7),
-    ("a", 12), ("h", 13), ("o", 12), ("o", 4), ("w", 9), ("a", 9), ("h", 15), ("o", 9), ("w", 5), ("h", 1),
-    ("w", 3), ("o", 10), ("a", 0), ("a", 5), ("w", 7), ("a", 3), ("w", 13), ("w", 11), ("a", 13), ("a", 7),
-    ("p", 14), ("h", 8), ("w", 15), ("a", 15), ("o", 15), ("o", 13), ("o", 3), ("w", 1), ("w", 8), ("a", 8),
-    ("o", 8), ("o", 7), ("o", 5), ("a", 11), ("p", 13), ("o", 11), ("a", 1), ("h", 14), ("m", 9), ("w", 14),
-    ("a", 14), ("o", 1), ("p", 7), ("m", 8), ("h", 6), ("o", 14), ("m", 3), ("w", 6), ("a", 6), ("o", 6),
-    ("m", 11), ("m", 1), ("p", 2), ("p", 11), ("m", 14), ("p", 6), ("o", 0), ("m", 6),
+    ("h", 0), ("p", 1), ("c", 0), ("p", 0), ("p", 2), ("p", 3), ("p", 4), ("w", 0), ("p", 5), ("p", 11),
+    ("p", 6), ("p", 7), ("p", 8), ("p", 9), ("p", 10), ("h", 2), ("h", 10), ("a", 0), ("h", 4), ("h", 12),
+    ("p", 12), ("p", 13), ("p", 14), ("p", 15), ("w", 2), ("h", 1), ("o", 0), ("a", 2), ("h", 9), ("h", 11),
+    ("w", 10), ("h", 3), ("w", 4), ("o", 2), ("a", 4), ("w", 12), ("o", 4), ("h", 5), ("h", 13), ("a", 12),
+    ("o", 12), ("h", 7), ("a", 10), ("h", 15), ("o", 10), ("w", 3), ("w", 11), ("a", 3), ("w", 9), ("w", 1),
+    ("a", 11), ("a", 1), ("w", 5), ("o", 3), ("o", 1), ("w", 13), ("a", 5), ("w", 7), ("a", 7), ("o", 7),
+    ("h", 14), ("w", 15), ("h", 6), ("a", 15), ("o", 5), ("h", 8), ("o", 15), ("a", 13), ("w", 6), ("o", 13),
+    ("m", 3), ("o", 11), ("w", 14), ("m", 1), ("w", 8), ("a", 8), ("o", 8), ("a", 6), ("a", 14), ("a", 9),
+    ("o", 6), ("o", 9), ("m", 11), ("o", 14), ("m", 8), ("m", 9), ("m", 14), ("m", 6),
 )
 
 

time: 51.3 us -> 50.5 us (0.984)
  the two profiles are of different devices: /device:TPU:44 before, /device:TPU:24 now
where the time goes in v6:
time: 50.5 us; the launch traced here: 50 us
  Pallas kernels  48.7 us (96%)
  between operations  0.66 us (1%)
  local copies, waits for them, and re-layouts  0.63 us (1%)
    pallas_call x1, Pallas kernels, on_device(): pl.pallas_call(kernel, out_shape=pltpu.VMEM((BEAMS, HEADS * HD), F32), in...  48.7 us

profile of v6, /device:TPU:24, one launch (start us, length us, event | category | flops | bytes accessed | tf_op | source)
XLA Modules:
  0.0 50.0 jit_solution(6821757204428497831)
XLA Ops:
  0.7 48.7 %carried_queries.1 = f32[16,1024]{1,0:T(8,128)S(1)} custom-call(s32[1]{0:T(128)S(6)} %copy.9.length_ref, bf16[16,1024]{1,0:T(8,128)(2,1)} %q_hbm.1, bf16[4096,256]{1,0:T(8,128)(2,1)} %bitcast.4, bf16[32,64,256]{2,1,0:T(8,128)(2,1)} %bitcast.5, s32[4,512]{1,0:T(4,128)} %bitcast.6, s32[1,512]{1,0:T(1,128)} %bitcast.7), custom_call_target="tpu_custom_call" | custom-call | tf_op jit(solution)/shard_map/carried_queries/pallas_call | solution.py:410
  49.3 0.6 %copy.8 = f32[16,1024]{1,0:T(8,128)} copy(f32[16,1024]{1,0:T(8,128)S(1)} %carried_queries.1) | data formatting | bytes 131072
